TPU v7x, 256 devices: a whole 4x4x8 slice. The times are simulated.
256 devices in a mesh: rows: 256 (over z, y, x, core).
Axes of the slice: x: 4, y: 4, z: 8, core: 2. Of those that a mesh axis runs over, the one named last changes fastest.
Arguments:
- genotypes: bfloat16 [131072, 8192], P('rows'), may hold values from -40 to 40
- probes: bfloat16 [8192, 64], replicated, may hold values from -0.00018310547 to 0.00018310547
Outputs:
- projected: float32 [8192, 64], P('rows')
- r_factor: float32 [64, 64], replicated
All inputs are finite; a program needn't handle non-finite values.
Results may differ from a plain program's by a relative error of at most 0.00045.
Values sent between devices are 32-bit elements; how exact they have to be, the bound alone decides.
A program may use at most 64 MiB of HBM per device.

v0:
```python
import jax
import jax.numpy as jnp
from jax import lax
from jax.sharding import PartitionSpec as P


def upper_inverse(r_factor):
    order = r_factor.shape[0]
    identity_mat = jnp.eye(order, dtype=jnp.float32)

    def one_row(turn, inverse):
        row_index = order - 1 - turn
        r_row = lax.dynamic_slice_in_dim(r_factor, row_index, 1, 0)
        unit_row = lax.dynamic_slice_in_dim(identity_mat, row_index, 1, 0)
        pivot = lax.dynamic_slice(r_factor, (row_index, row_index), (1, 1))
        new_row = (unit_row - jnp.dot(r_row, inverse, precision=lax.Precision.HIGHEST)) / pivot
        return lax.dynamic_update_slice_in_dim(inverse, new_row, row_index, 0)

    return lax.fori_loop(0, order, one_row, jnp.zeros((order, order), jnp.float32))


def on_device(genotypes, probes):
    sketch = jnp.dot(genotypes, probes, preferred_element_type=jnp.float32)
    local_gram = lax.dot_general(
        sketch, sketch, (((0,), (0,)), ((), ())), precision=lax.Precision.HIGHEST
    )
    total_gram = lax.psum(local_gram, "rows")
    r_factor = jnp.linalg.cholesky(total_gram).T
    inverse_factor = upper_inverse(r_factor)
    ortho_basis = jnp.dot(sketch, inverse_factor, precision=lax.Precision.HIGHEST)
    column_block = genotypes.astype(jnp.float32)
    projected = lax.psum_scatter(
        lax.dot_general(
            column_block, ortho_basis, (((0,), (0,)), ((), ())), precision=lax.Precision.HIGHEST
        ),
        "rows",
        scatter_dimension=0,
        tiled=True,
    )
    return (projected, r_factor)


def solution(mesh):
    return jax.shard_map(
        on_device,
        mesh=mesh,
        in_specs=(P("rows", None), P()),
        out_specs=(P("rows", None), P()),
        check_vma=False,
    )
```

profile of v0, /device:TPU:1, one launch (start us, length us, event | category | flops | bytes accessed | tf_op | source)
XLA Modules:
  0.0 1475.1 jit_solution(16447720768490849288)
XLA Ops:
  7.2 1.2 copy-done
  8.4 6.0 fusion.6
  14.7 81.5 %psum.7 = f32[64,64]{0,1:T(8,128)S(1)} all-reduce(f32[64,64]{0,1:T(8,128)S(1)} %fusion.7), channel_id=1, replica_groups=mesh['rows'=256] {'rows'}, use_global_device_ids=true, to_apply=%region_0.0 | all-reduce | flops 4096 | bytes 32768 | tf_op jit(solution)/shard_map/psum | solution.py:27
  96.3 5.8 cholesky.19
  103.6 90.7 %while.15 = (s32[]{:T(128)}, f32[64,64]{1,0:T(8,128)S(1)}, f32[64,64]{1,0:T(8,128)S(1)}, f32[64,64]{1,0:T(8,128)S(1)}, s32[]{:T(128)}, /*index=5*/s32[]{:T(128)}, s32[]{:T(128)}, s32[]{:T(128)}) while((s32[]{:T(128)}, f32[64,64]{1,0:T(8,128)S(1)}, f32[64,64]{1,0:T(8,128)S(1)}, f32[64,64]{1,0:T(8,128)S(1)}, s32[]{:T(128)}, ...), condition=%wide.region_4.5_spmd, body=%wide.region_3.4_spmd.sunk | while | flops 49286 | bytes 35743 | solution.py:19
  104.2 0.8 fusion.23
  105.6 0.8 fusion.23
  107.0 0.8 fusion.23
  109.8 0.8 fusion.23
  111.3 0.8 fusion.23
  115.5 0.8 fusion.23
  116.9 0.8 fusion.23
  121.2 0.8 fusion.23
  122.6 0.8 fusion.23
  125.4 0.8 fusion.23
  126.9 0.8 fusion.23
  128.3 0.8 fusion.23
  131.1 0.8 fusion.23
  132.5 0.8 fusion.23
  133.9 0.8 fusion.23
  136.8 0.8 fusion.23
  138.2 0.8 fusion.23
  142.5 0.8 fusion.23
  143.9 0.8 fusion.23
  148.1 0.8 fusion.23
  149.5 0.8 fusion.23
  152.4 0.8 fusion.23
  153.8 0.8 fusion.23
  155.2 0.8 fusion.23
  194.9 7.0 convolution_bitcast_fusion
  201.9 2.7 copy.15
  204.7 1263.6 %reduce-scatter.4.cloned.1.call-done = f32[32,64]{1,0:T(8,128)} async-done(((f32[8192,64]{1,0:T(8,128)}), f32[32,64]{1,0:T(8,128)}) %reduce-scatter.4.cloned.1.call-update) | async-done | bytes 8208
  (183 shorter events, 73.0 us)
Async XLA Ops:
  7.2 1.2 copy-start
  7.2 1461.1 %reduce-scatter.4.cloned.1.call-start = ((), (), s32[]{:S(2)}) async-start(), calls=%async_computation.1 | async-start | bytes 4210688
  194.3 10.3 copy-start.1
Sparse Core Ops, SparseCore 0:
  204.8 1263.4 reduce-scatter.3
where the time goes:
time: 1480 us
  waiting for transfers between devices  1260 us (85%)
  blocking collectives  81.5 us (6%)
  matrix products  63.9 us (4%)
  local copies, waits for them, and re-layouts  43.3 us (3%)
    unnamed x2, waiting for transfers between devices  1260 us
    psum x1, blocking collectives, on_device(): total_gram = lax.psum(local_gram, 'rows')  81.5 us
    dot_general x64, matrix products, one_row(): jnp.dot(r_row, inverse, precision=lax.Precision.HIGHEST)  50 us
    dynamic_slice x64, local copies, waits for them, and re-layouts, one_row(): pivot = lax.dynamic_slice(r_factor, (row_index, row_index), (1, 1))  37.7 us
  transfers between devices with their start and end apart: 1, of which 1 were waited for; matrix products, arithmetic and copies ran while one was open for 0% of the time, Pallas kernels for 0%

commit v1 on v0

v1 whole, which is shorter than its diff:
```python
import functools

import jax
import jax.numpy as jnp
from jax import lax
from jax.experimental import pallas as pl
from jax.experimental.pallas import tpu as pltpu
from jax.sharding import PartitionSpec as P

pinned = pltpu.with_memory_space_constraint
MESH = pl.DeviceIdType.MESH
F32 = jnp.float32
BF16 = jnp.bfloat16
NT = (((1,), (1,)), ((), ()))
PROBES = 64
CHUNKS = 8
VMEM_LIMIT = 48 * 2**20
DEPTH = 4
PANEL = 8
OFFSETS = {8: (4, 3, 5, 2, 6, 1, 7, 0), 4: (2, 1, 3, 0), 2: (1, 0)}
SCHEDULE = (
    "meet", "gram", "project0", "project1", "gramC", "project2", "near0", "project3", "near1",
    "near2", "near3", "plane0", "gramXY", "plane1", "plane2", "plane3", "axis0", "axis1",
    "gramZ", "axis2", "axis3", "gramAll", "factor", "finish",
)


def split3(value):
    high = value.astype(BF16)
    rest = value - high.astype(F32)
    middle = rest.astype(BF16)
    low = (rest - middle.astype(F32)).astype(BF16)
    return high, middle, low


def factor_panel(below, base):
    size = below.shape[0]
    cols = [jnp.broadcast_to(below[:, base + q : base + q + 1], (size, 128)) for q in range(PANEL)]
    rows = [below[q : q + 1] for q in range(PANEL)]
    for q in range(PANEL):
        pivot = cols[q][q : q + 1]
        scale = lax.rsqrt(pivot)
        scale = scale * (1.5 - 0.5 * pivot * scale * scale)
        cols[q] = cols[q] * scale
        rows[q] = rows[q] * scale
        for later in range(q + 1, PANEL):
            factor = cols[q][later : later + 1]
            cols[later] = cols[later] - cols[q] * factor
            rows[later] = rows[later] - rows[q] * factor
    rest = None
    if size > PANEL:
        rest = below[PANEL:]
        for q in range(PANEL):
            rest = rest - cols[q][PANEL:] * rows[q]
    return jnp.concatenate(rows, axis=0), rest


def finish_kernel(sum_ref, work_ref, projected_ref, r_ref):
    full = work_ref[...]
    row = lax.broadcasted_iota(jnp.int32, full.shape, 0)
    lane = lax.broadcasted_iota(jnp.int32, full.shape, 1)
    r_ref[...] = jnp.where(lane >= row, full, 0.0)[:, :PROBES]
    high = jnp.where(lane >= PROBES, full, 0.0)
    low = pltpu.roll(high, PROBES, 1)
    for half, inverse in enumerate((low, high)):
        projected_ref[pl.ds(16 * half, 16)] = lax.dot_general(
            sum_ref[...], inverse, NT, precision=lax.Precision.HIGHEST, preferred_element_type=F32
        )


def kernel(sizes, schedule, g_hbm, p_hbm, sum_ref, work_ref, g_buf, p_buf, split, ya, yb, ca, cb,
           ra1, rb1, sa1, sb1, ra2, rb2, total2, rz, gram_own, gram_c, gram_xy, gram_z, gram_all, work,
           load_sem, core_send, core_recv, one_send, one_recv, two_send, two_recv,
           z_send, z_recv, gram_send, gram_recv):
    nz, ny, nx = sizes
    groups = nz // 2
    offsets = OFFSETS[nz]
    me = lax.axis_index("rows")
    core = lax.rem(me, 2)
    x = lax.rem(me // 2, nx)
    y = lax.rem(me // (2 * nx), ny)
    z = me // (2 * nx * ny)

    def device(z=z, y=y, x=x, core=core):
        return (((z * ny + y) * nx + x) * 2 + core,)

    def ahead(position, offset, size):
        return lax.rem(position + offset, size)

    barrier = pltpu.get_barrier_semaphore()
    peers = [device(core=1 - core)]
    others = [(dy, dx) for dy in range(ny) for dx in range(nx) if dy or dx]
    others.sort(key=lambda d: -min(d[0], ny - d[0]) - min(d[1], nx - d[1]))
    peers += [device(y=ahead(y, dy, ny), x=ahead(x, dx, nx)) for dy, dx in others]
    peers += [device(z=ahead(z, o, nz)) for o in range(1, nz)]
    for peer in peers:
        pl.semaphore_signal(barrier, inc=1, device_id=peer, device_id_type=MESH)

    columns = g_hbm.shape[1] // CHUNKS

    def part(j):
        return (slice(None), pl.ds(j * columns, columns))

    loads = [
        [pltpu.make_async_copy(p_hbm.at[part(j)], p_buf.at[part(j)], load_sem.at[0, j]),
         pltpu.make_async_copy(g_hbm.at[part(j)], g_buf.at[part(j)], load_sem.at[1, j])]
        for j in range(CHUNKS)
    ]
    for pair in loads[:DEPTH]:
        for load in pair:
            load.start()
    sketch = jnp.zeros((PROBES, g_hbm.shape[0]), F32)
    for j in range(CHUNKS):
        for load in loads[j]:
            load.wait()
        if j + DEPTH < CHUNKS:
            for load in loads[j + DEPTH]:
                load.start()
        sketch += lax.dot_general(p_buf[part(j)], g_buf[part(j)], NT, preferred_element_type=F32)
    pieces = split3(sketch)
    for i, piece in enumerate(pieces):
        split[pl.ds(i * PROBES, PROBES)] = piece

    sent = []

    def copy(src, dst, send_sem, recv_sem, to):
        done = pltpu.make_async_remote_copy(
            src_ref=src, dst_ref=dst, send_sem=send_sem, recv_sem=recv_sem,
            device_id=to, device_id_type=MESH,
        )
        done.start()
        sent.append(done)
        return done

    left = lax.broadcasted_iota(jnp.int32, (16, 128), 1) < PROBES
    pending = {}

    def spread(buffer, mine, targets, sem0):
        return [
            copy(buffer.at[mine], buffer.at[mine], gram_send.at[sem0 + i], gram_recv.at[sem0 + i], to)
            for i, to in enumerate(targets)
        ]

    def total(arrived):
        for done in pending["gram"]:
            done.wait_recv()
        value = arrived[0]
        for i in range(1, arrived.shape[0]):
            value = value + arrived[i]
        return value

    def meet():
        pl.semaphore_wait(barrier, len(peers))

    def gram():
        full = split[...]
        product = sum(
            lax.dot_general(full, piece, NT, preferred_element_type=F32) for piece in pieces[::-1]
        )
        product = product[2 * PROBES :] + product[PROBES : 2 * PROBES] + product[:PROBES]
        packed = jnp.concatenate([product[:32], product[32:]], axis=1)
        gram_own[...] = packed.reshape(2, 16, 128)
        gram_c[core] = gram_own[core]
        pending["gram"] = [
            copy(gram_own.at[1 - core], gram_c.at[core], gram_send.at[0], gram_recv.at[0],
                 device(core=1 - core))
        ]

    def gram_core():
        mine = y * nx + x
        gram_xy[mine] = total(gram_c)
        to = [device(y=ahead(y, dy, ny), x=ahead(x, dx, nx)) for dy, dx in others]
        pending["gram"] = spread(gram_xy, mine, to, 1)

    def gram_plane():
        gram_z[z] = total(gram_xy)
        far = sorted(range(1, nz), key=lambda o: -min(o, nz - o))
        to = [device(z=ahead(z, o, nz)) for o in far]
        pending["gram"] = spread(gram_z, z, to, nx * ny)

    def gram_axis():
        gram_all[core] = total(gram_z)
        pending["gram"] = spread(gram_all, core, [device(core=1 - core)], nx * ny + nz - 1)

    def gram_whole():
        for done in pending["gram"]:
            done.wait_recv()
        value = gram_all[...].reshape(32, 128)
        row = lax.broadcasted_iota(jnp.int32, (32, 128), 0)
        lane = lax.broadcasted_iota(jnp.int32, (32, 128), 1)
        upper = jnp.where(lane == row + PROBES, 1.0, 0.0)
        lower = jnp.where(lane == row + PROBES + 32, 1.0, 0.0)
        work[:32] = jnp.where(lane < PROBES, value, upper)
        work[32:] = jnp.where(lane < PROBES, pltpu.roll(value, PROBES, 1), lower)

    def factor():
        rest = work[...]
        for base in range(0, PROBES, PANEL):
            done, rest = factor_panel(rest, base)
            work_ref[pl.ds(base, PANEL)] = done

    def project(g):
        for zz in range(2):
            z_to = ahead(z, offsets[2 * g + zz], nz)
            for y_to in range(ny):
                start = pl.multiple_of((z_to * ny + y_to) * 256, 256)
                out = jnp.dot(split[...], g_buf[:, pl.ds(start, 256)], preferred_element_type=F32)
                out = out[2 * PROBES :] + out[PROBES : 2 * PROBES] + out[:PROBES]
                turned = jnp.concatenate([out[:, :128], out[:, 128:]], axis=0).T
                for x_low in range(2):
                    for c in range(2):
                        at = 64 * x_low + 32 * c
                        top, bottom = turned[at : at + 16], turned[at + 16 : at + 32]
                        low = jnp.where(left, top, pltpu.roll(bottom, PROBES, 1))
                        high = jnp.where(left, pltpu.roll(top, PROBES, 1), bottom)
                        for x_to, block in ((x_low, low), (x_low + 2, high)):
                            ya[c, g, x_to, 2 * y_to + zz] = block[:8]
                            yb[c, g, y_to, 2 * x_to + zz] = block[8:]
        to = device(core=1 - core)
        pending["core", g] = [
            copy(ya.at[1 - core, g], ca.at[g], core_send.at[g, 0], core_recv.at[g, 0], to),
            copy(yb.at[1 - core, g], cb.at[g], core_send.at[g, 1], core_recv.at[g, 1], to),
        ]

    def near(g):
        from_a, from_b = pending["core", g]
        from_a.wait_recv()
        ya[core, g] = ya[core, g] + ca[g]
        first = [
            copy(ya.at[core, g, ahead(x, o, nx)], ra1.at[g, o - 1],
                 one_send.at[g, 0, o - 1], one_recv.at[g, 0, o - 1], device(x=ahead(x, o, nx)))
            for o in range(1, nx)
        ]
        from_b.wait_recv()
        yb[core, g] = yb[core, g] + cb[g]
        second = [
            copy(yb.at[core, g, ahead(y, o, ny)], rb1.at[g, o - 1],
                 one_send.at[g, 1, o - 1], one_recv.at[g, 1, o - 1], device(y=ahead(y, o, ny)))
            for o in range(1, ny)
        ]
        pending["one", g] = first, second

    def plane(g):
        first, second = pending["one", g]
        for done in first:
            done.wait_recv()
        value = ya[core, g, x]
        for o in range(1, nx):
            value = value + ra1[g, o - 1]
        sa1[g] = value
        first = [
            copy(sa1.at[g, pl.ds(2 * ahead(y, o, ny), 2)], ra2.at[g, o - 1],
                 two_send.at[g, 0, o - 1], two_recv.at[g, 0, o - 1], device(y=ahead(y, o, ny)))
            for o in range(1, ny)
        ]
        for done in second:
            done.wait_recv()
        value = yb[core, g, y]
        for o in range(1, ny):
            value = value + rb1[g, o - 1]
        sb1[g] = value
        second = [
            copy(sb1.at[g, pl.ds(2 * ahead(x, o, nx), 2)], rb2.at[g, o - 1],
                 two_send.at[g, 1, o - 1], two_recv.at[g, 1, o - 1], device(x=ahead(x, o, nx)))
            for o in range(1, nx)
        ]
        pending["two", g] = first, second

    pending["z"] = []

    def axis(g):
        first, second = pending["two", g]
        for done in first + second:
            done.wait_recv()
        value_a = sa1[g, pl.ds(2 * y, 2)]
        for o in range(1, ny):
            value_a = value_a + ra2[g, o - 1]
        value_b = sb1[g, pl.ds(2 * x, 2)]
        for o in range(1, nx):
            value_b = value_b + rb2[g, o - 1]
        for zz in range(2):
            slot = 2 * g + zz
            total2[slot, 0] = value_a[zz]
            total2[slot, 1] = value_b[zz]
            if offsets[slot]:
                pending["z"].append(
                    copy(total2.at[slot], rz.at[slot], z_send.at[slot], z_recv.at[slot],
                         device(z=ahead(z, offsets[slot], nz)))
                )

    def finish():
        for done in pending["z"]:
            done.wait_recv()
        value = total2[nz - 1]
        for slot in range(nz - 1):
            value = value + rz[slot]
        sum_ref[...] = value.reshape(16, 128)

    steps = {
        "meet": meet, "gram": gram, "gramC": gram_core, "gramXY": gram_plane, "gramZ": gram_axis,
        "gramAll": gram_whole, "factor": factor, "finish": finish,
    }
    for g in range(groups):
        steps[f"project{g}"] = functools.partial(project, g)
        steps[f"near{g}"] = functools.partial(near, g)
        steps[f"plane{g}"] = functools.partial(plane, g)
        steps[f"axis{g}"] = functools.partial(axis, g)
    for step in schedule:
        if step in steps:
            steps[step]()
    for done in sent:
        done.wait_send()


def build(mesh, sizes, schedule=SCHEDULE):
    nz, ny, nx = sizes
    groups = nz // 2

    def step(genotypes, probes):
        samples, markers = genotypes.shape
        vmem = pltpu.VMEM
        scratch = [
            vmem((samples, markers), BF16),
            vmem((PROBES, markers), BF16),
            vmem((3 * PROBES, samples), BF16),
            vmem((2, groups, nx, 2 * ny, 8, 128), F32),
            vmem((2, groups, ny, 2 * nx, 8, 128), F32),
            vmem((groups, nx, 2 * ny, 8, 128), F32),
            vmem((groups, ny, 2 * nx, 8, 128), F32),
            vmem((groups, max(nx - 1, 1), 2 * ny, 8, 128), F32),
            vmem((groups, max(ny - 1, 1), 2 * nx, 8, 128), F32),
            vmem((groups, 2 * ny, 8, 128), F32),
            vmem((groups, 2 * nx, 8, 128), F32),
            vmem((groups, max(ny - 1, 1), 2, 8, 128), F32),
            vmem((groups, max(nx - 1, 1), 2, 8, 128), F32),
            vmem((nz, 2, 8, 128), F32),
            vmem((nz - 1, 2, 8, 128), F32),
            vmem((2, 16, 128), F32),
            vmem((2, 16, 128), F32),
            vmem((ny * nx, 16, 128), F32),
            vmem((nz, 16, 128), F32),
            vmem((2, 16, 128), F32),
            vmem((PROBES, 128), F32),
            pltpu.SemaphoreType.DMA((2, CHUNKS)),
        ]
        most = max(nx, ny) - 1
        for shape in ((groups, 2), (groups, 2, most), (groups, 2, most), (nz,), (nx * ny + nz,)):
            scratch += [pltpu.SemaphoreType.DMA(shape)] * 2
        whole = pl.BlockSpec(memory_space=pltpu.VMEM)
        summed, factors = pl.pallas_call(
            functools.partial(kernel, sizes, schedule),
            out_shape=(
                jax.ShapeDtypeStruct((16, 128), F32),
                jax.ShapeDtypeStruct((PROBES, 128), F32),
            ),
            in_specs=[pl.BlockSpec(memory_space=pltpu.HBM)] * 2,
            out_specs=(whole, whole),
            scratch_shapes=scratch,
            compiler_params=pltpu.CompilerParams(
                collective_id=0, has_side_effects=True, vmem_limit_bytes=VMEM_LIMIT
            ),
            name="range_finder",
        )(pinned(genotypes, pltpu.HBM), pinned(probes.T, pltpu.HBM))
        return pl.pallas_call(
            finish_kernel,
            out_shape=(
                jax.ShapeDtypeStruct((32, PROBES), F32),
                jax.ShapeDtypeStruct((PROBES, PROBES), F32),
            ),
            in_specs=[whole, whole],
            out_specs=(whole, whole),
            compiler_params=pltpu.CompilerParams(vmem_limit_bytes=4 * 2**20),
            name="finish",
        )(summed, factors)

    return jax.shard_map(
        step,
        mesh=mesh,
        in_specs=(P("rows", None), P()),
        out_specs=(P("rows", None), P()),
        check_vma=False,
    )


def solution(mesh):
    return build(mesh, (8, 4, 4))
```

time: 1480 us -> 32.4 us (0.02)
  waiting for transfers between devices: 1260 us -> 0 us
  blocking collectives: 81.5 us -> 0 us
  matrix products: 63.9 us -> 0 us
  local copies, waits for them, and re-layouts: 43.3 us -> 0 us
  Pallas kernels: 0 us -> 31.6 us
    unnamed x2 -> x0, waiting for transfers between devices: 1260 us -> none
    psum x1 -> x0, blocking collectives: 81.5 us -> none  [on_device(): total_gram = lax.psum(local_gram, 'rows')]
    dot_general x68 -> x0, matrix products: 63.9 us -> none  [the longest x64 50 us: one_row(): jnp.dot(r_row, inverse, precision=lax.Precision.HIGHEST)]
    dynamic_slice x64 -> x0, local copies, waits for them, and re-layouts: 37.7 us -> none  [one_row(): pivot = lax.dynamic_slice(r_factor, (row_index, row_index), (1, 1))]
    pallas_call x0 -> x2, Pallas kernels: none -> 31.6 us  [the longest x1 30.7 us: step(): pl.pallas_call(functools.partial(kernel, sizes, schedule), out_shape=(jax...]
  transfers between devices with their start and end apart: 1 -> 0, of which waited for: 1 -> 0; matrix products, arithmetic and copies ran while one was open for 0% -> 0% of each run, Pallas kernels for 0% -> 0%
where the time goes in v1:
time: 32.4 us; the launch traced here: 32.3 us
  Pallas kernels  31.6 us (98%)
  between operations  0.64 us (2%)
    pallas_call x1, Pallas kernels, step(): pl.pallas_call(functools.partial(kernel, sizes, schedule), out_shape=(jax...  30.7 us
    pallas_call x1, Pallas kernels, step(): pl.pallas_call(finish_kernel, out_shape=(jax.ShapeDtypeStruct((32, PROBES...  0.9 us

profile of v1, /device:TPU:1, one launch (start us, length us, event | category | flops | bytes accessed | tf_op | source)
XLA Modules:
  0.0 32.3 jit_solution(8541627919648579426)
XLA Ops:
  0.6 30.7 %range_finder.1 = (f32[16,128]{1,0:T(8,128)S(1)}, f32[64,128]{1,0:T(8,128)S(1)}) custom-call(bf16[512,8192]{1,0:T(8,128)(2,1)} %g_hbm.1, bf16[64,8192]{1,0:T(8,128)(2,1)} %bitcast.1), custom_call_target="tpu_custom_call" | custom-call | tf_op jit(solution)/shard_map/range_finder/pallas_call | solution.py:350
  31.4 0.9 %finish.1 = (f32[32,64]{1,0:T(8,128)}, f32[64,64]{1,0:T(8,128)}) custom-call(f32[16,128]{1,0:T(8,128)S(1)} %get-tuple-element.4.sum_ref, f32[64,128]{1,0:T(8,128)S(1)} %get-tuple-element.5.work_ref), custom_call_target="tpu_custom_call" | custom-call | tf_op jit(solution)/shard_map/finish/pallas_call | solution.py:364

commit v2 on v1

--- a/solution.py
+++ b/solution.py
@@ -15,14 +15,20 @@
 PROBES = 64
 CHUNKS = 8
 VMEM_LIMIT = 48 * 2**20
-DEPTH = 4
+DEPTH = 5
 PANEL = 8
-OFFSETS = {8: (4, 3, 5, 2, 6, 1, 7, 0), 4: (2, 1, 3, 0), 2: (1, 0)}
-SCHEDULE = (
-    "meet", "gram", "project0", "project1", "gramC", "project2", "near0", "project3", "near1",
-    "near2", "near3", "plane0", "gramXY", "plane1", "plane2", "plane3", "axis0", "axis1",
-    "gramZ", "axis2", "axis3", "gramAll", "factor", "finish",
-)
+OFFSETS = {8: (4, 3, 5, 2, 6, 1, 7, 0), 4: (2, 1, 3, 0)}
+NEAREST = {8: (0, 0), 4: (1, 3)}
+BATCHES = {8: ((0, 2), (2, 4), (4, 6), (6, 8)), 4: ((0, 1), (1, 3), (3, 4))}
+UNITS = {8: ((0, 2), (2, 4), (4, 6), (6, 8)), 4: ((0, 1), (3, 4))}
+SCHEDULES = {
+    8: ("meet", "gram", "project0", "gramC", "project1", "near0", "project2", "near1", "project3", "near2", "near3", "plane0", "gramXY", "plane1", "plane2", "axis0", "plane3", "axis1", "gramZ", "axis2", "axis3", "gramAll", "factor", "finish",
+    ),
+    4: (
+        "meet", "gram", "project0", "project1", "project2", "gramC", "near0", "along", "gramXY",
+        "near1", "plane0", "plane1", "axis0", "axis1", "gramZ", "gramAll", "factor", "finish",
+    ),
+}
 
 
 def split3(value):
@@ -69,12 +75,14 @@
 
 
 def kernel(sizes, schedule, g_hbm, p_hbm, sum_ref, work_ref, g_buf, p_buf, split, ya, yb, ca, cb,
-           ra1, rb1, sa1, sb1, ra2, rb2, total2, rz, gram_own, gram_c, gram_xy, gram_z, gram_all, work,
-           load_sem, core_send, core_recv, one_send, one_recv, two_send, two_recv,
+           za, zb, ra1, rb1, sa1, sb1, ra2, rb2, total2, rz, gram_own, gram_c, gram_xy, gram_z, gram_all, work,
+           load_sem, core_send, core_recv, along_send, along_recv, one_send, one_recv, two_send, two_recv,
            z_send, z_recv, gram_send, gram_recv):
     nz, ny, nx = sizes
-    groups = nz // 2
     offsets = OFFSETS[nz]
+    nearest = NEAREST[nz]
+    batches = BATCHES[nz]
+    units = UNITS[nz]
     me = lax.axis_index("rows")
     core = lax.rem(me, 2)
     x = lax.rem(me // 2, nx)
@@ -87,6 +95,19 @@
     def ahead(position, offset, size):
         return lax.rem(position + offset, size)
 
+    columns = g_hbm.shape[1] // CHUNKS
+
+    def part(j):
+        return (slice(None), pl.ds(j * columns, columns))
+
+    loads = [
+        [pltpu.make_async_copy(p_hbm.at[part(j)], p_buf.at[part(j)], load_sem.at[0, j]),
+         pltpu.make_async_copy(g_hbm.at[part(j)], g_buf.at[part(j)], load_sem.at[1, j])]
+        for j in range(CHUNKS)
+    ]
+    for pair in loads[:DEPTH]:
+        for load in pair:
+            load.start()
     barrier = pltpu.get_barrier_semaphore()
     peers = [device(core=1 - core)]
     others = [(dy, dx) for dy in range(ny) for dx in range(nx) if dy or dx]
@@ -96,19 +117,6 @@
     for peer in peers:
         pl.semaphore_signal(barrier, inc=1, device_id=peer, device_id_type=MESH)
 
-    columns = g_hbm.shape[1] // CHUNKS
-
-    def part(j):
-        return (slice(None), pl.ds(j * columns, columns))
-
-    loads = [
-        [pltpu.make_async_copy(p_hbm.at[part(j)], p_buf.at[part(j)], load_sem.at[0, j]),
-         pltpu.make_async_copy(g_hbm.at[part(j)], g_buf.at[part(j)], load_sem.at[1, j])]
-        for j in range(CHUNKS)
-    ]
-    for pair in loads[:DEPTH]:
-        for load in pair:
-            load.start()
     sketch = jnp.zeros((PROBES, g_hbm.shape[0]), F32)
     for j in range(CHUNKS):
         for load in loads[j]:
@@ -199,9 +207,10 @@
             done, rest = factor_panel(rest, base)
             work_ref[pl.ds(base, PANEL)] = done
 
-    def project(g):
-        for zz in range(2):
-            z_to = ahead(z, offsets[2 * g + zz], nz)
+    def project(i):
+        first, last = batches[i]
+        for slot in range(first, last):
+            z_to = ahead(z, offsets[slot], nz)
             for y_to in range(ny):
                 start = pl.multiple_of((z_to * ny + y_to) * 256, 256)
                 out = jnp.dot(split[...], g_buf[:, pl.ds(start, 256)], preferred_element_type=F32)
@@ -214,85 +223,104 @@
                         low = jnp.where(left, top, pltpu.roll(bottom, PROBES, 1))
                         high = jnp.where(left, pltpu.roll(top, PROBES, 1), bottom)
                         for x_to, block in ((x_low, low), (x_low + 2, high)):
-                            ya[c, g, x_to, 2 * y_to + zz] = block[:8]
-                            yb[c, g, y_to, 2 * x_to + zz] = block[8:]
+                            ya[c, slot, x_to, y_to] = block[:8]
+                            yb[c, slot, y_to, x_to] = block[8:]
         to = device(core=1 - core)
-        pending["core", g] = [
-            copy(ya.at[1 - core, g], ca.at[g], core_send.at[g, 0], core_recv.at[g, 0], to),
-            copy(yb.at[1 - core, g], cb.at[g], core_send.at[g, 1], core_recv.at[g, 1], to),
+        slots = pl.ds(first, last - first)
+        pending["core", i] = [
+            copy(ya.at[1 - core, slots], ca.at[slots], core_send.at[i, 0], core_recv.at[i, 0], to),
+            copy(yb.at[1 - core, slots], cb.at[slots], core_send.at[i, 1], core_recv.at[i, 1], to),
         ]
 
-    def near(g):
-        from_a, from_b = pending["core", g]
-        from_a.wait_recv()
-        ya[core, g] = ya[core, g] + ca[g]
-        first = [
-            copy(ya.at[core, g, ahead(x, o, nx)], ra1.at[g, o - 1],
-                 one_send.at[g, 0, o - 1], one_recv.at[g, 0, o - 1], device(x=ahead(x, o, nx)))
-            for o in range(1, nx)
-        ]
-        from_b.wait_recv()
-        yb[core, g] = yb[core, g] + cb[g]
-        second = [
-            copy(yb.at[core, g, ahead(y, o, ny)], rb1.at[g, o - 1],
-                 one_send.at[g, 1, o - 1], one_recv.at[g, 1, o - 1], device(y=ahead(y, o, ny)))
-            for o in range(1, ny)
-        ]
-        pending["one", g] = first, second
-
-    def plane(g):
-        first, second = pending["one", g]
-        for done in first:
+    def chip_sum(which, slots):
+        mine, other = ((ya, ca), (yb, cb))[which]
+        for i, (first, last) in enumerate(batches):
+            if first < slots[1] and slots[0] < last and (i, which) not in settled:
+                settled.add((i, which))
+                pending["core", i][which].wait_recv()
+        at = pl.ds(slots[0], slots[1] - slots[0])
+        mine[core, at] = mine[core, at] + other[at]
+
+    settled = set()
+
+    def along():
+        out = []
+        for which, (mine, landing) in enumerate(((ya, za), (yb, zb))):
+            chip_sum(which, nearest)
+            for i, slot in enumerate(range(*nearest)):
+                out.append(
+                    copy(mine.at[core, slot], landing.at[i], along_send.at[which, i],
+                         along_recv.at[which, i], device(z=ahead(z, offsets[slot], nz)))
+                )
+        pending["along"] = out
+
+    def near(i):
+        first, last = units[i]
+        slots = pl.ds(first, last - first)
+        out = []
+        for which, (mine, landing, size, here) in enumerate(((ya, ra1, nx, x), (yb, rb1, ny, y))):
+            chip_sum(which, units[i])
+            if last == nz and "along" in pending:
+                for done in pending["along"][2 * which : 2 * which + 2]:
+                    done.wait_recv()
+                arrived = (za, zb)[which]
+                mine[core, nz - 1] = mine[core, nz - 1] + (arrived[0] + arrived[1])
+            for o in (2, 1, 3) if size == 4 else range(1, size):
+                to_there = ahead(here, o, size)
+                to = device(x=to_there) if which == 0 else device(y=to_there)
+                out.append(
+                    copy(mine.at[core, slots, to_there], landing.at[slots, o - 1],
+                         one_send.at[i, which, o - 1], one_recv.at[i, which, o - 1], to)
+                )
+        pending["one", i] = out
+
+    def plane(i):
+        first, last = units[i]
+        slots = pl.ds(first, last - first)
+        arriving = pending["one", i]
+        out = []
+        for which, (mine, landed, kept, landing, size, here, size2, here2) in enumerate((
+            (ya, ra1, sa1, ra2, nx, x, ny, y), (yb, rb1, sb1, rb2, ny, y, nx, x),
+        )):
+            for done in arriving[: size - 1]:
+                done.wait_recv()
+            arriving = arriving[size - 1 :]
+            value = mine[core, slots, here]
+            for o in range(1, size):
+                value = value + landed[slots, o - 1]
+            kept[slots] = value
+            for o in (2, 1, 3) if size2 == 4 else range(1, size2):
+                to_there = ahead(here2, o, size2)
+                to = device(y=to_there) if which == 0 else device(x=to_there)
+                out.append(
+                    copy(kept.at[slots, to_there], landing.at[slots, o - 1],
+                         two_send.at[i, which, o - 1], two_recv.at[i, which, o - 1], to)
+                )
+        pending["two", i] = out
+
+    pending["z"] = []
+
+    def axis(i):
+        first, last = units[i]
+        slots = pl.ds(first, last - first)
+        for done in pending["two", i]:
             done.wait_recv()
-        value = ya[core, g, x]
-        for o in range(1, nx):
-            value = value + ra1[g, o - 1]
-        sa1[g] = value
-        first = [
-            copy(sa1.at[g, pl.ds(2 * ahead(y, o, ny), 2)], ra2.at[g, o - 1],
-                 two_send.at[g, 0, o - 1], two_recv.at[g, 0, o - 1], device(y=ahead(y, o, ny)))
-            for o in range(1, ny)
-        ]
-        for done in second:
-            done.wait_recv()
-        value = yb[core, g, y]
-        for o in range(1, ny):
-            value = value + rb1[g, o - 1]
-        sb1[g] = value
-        second = [
-            copy(sb1.at[g, pl.ds(2 * ahead(x, o, nx), 2)], rb2.at[g, o - 1],
-                 two_send.at[g, 1, o - 1], two_recv.at[g, 1, o - 1], device(x=ahead(x, o, nx)))
-            for o in range(1, nx)
-        ]
-        pending["two", g] = first, second
-
-    pending["z"] = []
-
-    def axis(g):
-        first, second = pending["two", g]
-        for done in first + second:
-            done.wait_recv()
-        value_a = sa1[g, pl.ds(2 * y, 2)]
-        for o in range(1, ny):
-            value_a = value_a + ra2[g, o - 1]
-        value_b = sb1[g, pl.ds(2 * x, 2)]
-        for o in range(1, nx):
-            value_b = value_b + rb2[g, o - 1]
-        for zz in range(2):
-            slot = 2 * g + zz
-            total2[slot, 0] = value_a[zz]
-            total2[slot, 1] = value_b[zz]
+        for which, (kept, landed, size, here) in enumerate(((sa1, ra2, ny, y), (sb1, rb2, nx, x))):
+            value = kept[slots, here]
+            for o in range(1, size):
+                value = value + landed[slots, o - 1]
+            total2[slots, which] = value
+        for slot in range(first, last):
             if offsets[slot]:
                 pending["z"].append(
-                    copy(total2.at[slot], rz.at[slot], z_send.at[slot], z_recv.at[slot],
-                         device(z=ahead(z, offsets[slot], nz)))
+                    (slot, copy(total2.at[slot], rz.at[slot], z_send.at[slot], z_recv.at[slot],
+                                device(z=ahead(z, offsets[slot], nz))))
                 )
 
     def finish():
-        for done in pending["z"]:
+        value = total2[nz - 1]
+        for slot, done in pending["z"]:
             done.wait_recv()
-        value = total2[nz - 1]
-        for slot in range(nz - 1):
             value = value + rz[slot]
         sum_ref[...] = value.reshape(16, 128)
 
@@ -300,11 +328,13 @@
         "meet": meet, "gram": gram, "gramC": gram_core, "gramXY": gram_plane, "gramZ": gram_axis,
         "gramAll": gram_whole, "factor": factor, "finish": finish,
     }
-    for g in range(groups):
-        steps[f"project{g}"] = functools.partial(project, g)
-        steps[f"near{g}"] = functools.partial(near, g)
-        steps[f"plane{g}"] = functools.partial(plane, g)
-        steps[f"axis{g}"] = functools.partial(axis, g)
+    steps["along"] = along
+    for i in range(len(batches)):
+        steps[f"project{i}"] = functools.partial(project, i)
+    for i in range(len(units)):
+        steps[f"near{i}"] = functools.partial(near, i)
+        steps[f"plane{i}"] = functools.partial(plane, i)
+        steps[f"axis{i}"] = functools.partial(axis, i)
     for step in schedule:
         if step in steps:
             steps[step]()
@@ -312,9 +342,9 @@
         done.wait_send()
 
 
-def build(mesh, sizes, schedule=SCHEDULE):
+def build(mesh, sizes):
     nz, ny, nx = sizes
-    groups = nz // 2
+    schedule = SCHEDULES[nz]
 
     def step(genotypes, probes):
         samples, markers = genotypes.shape
@@ -323,18 +353,20 @@
             vmem((samples, markers), BF16),
             vmem((PROBES, markers), BF16),
             vmem((3 * PROBES, samples), BF16),
-            vmem((2, groups, nx, 2 * ny, 8, 128), F32),
-            vmem((2, groups, ny, 2 * nx, 8, 128), F32),
-            vmem((groups, nx, 2 * ny, 8, 128), F32),
-            vmem((groups, ny, 2 * nx, 8, 128), F32),
-            vmem((groups, max(nx - 1, 1), 2 * ny, 8, 128), F32),
-            vmem((groups, max(ny - 1, 1), 2 * nx, 8, 128), F32),
-            vmem((groups, 2 * ny, 8, 128), F32),
-            vmem((groups, 2 * nx, 8, 128), F32),
-            vmem((groups, max(ny - 1, 1), 2, 8, 128), F32),
-            vmem((groups, max(nx - 1, 1), 2, 8, 128), F32),
+            vmem((2, nz, nx, ny, 8, 128), F32),
+            vmem((2, nz, ny, nx, 8, 128), F32),
+            vmem((nz, nx, ny, 8, 128), F32),
+            vmem((nz, ny, nx, 8, 128), F32),
+            vmem((2, nx, ny, 8, 128), F32),
+            vmem((2, ny, nx, 8, 128), F32),
+            vmem((nz, max(nx - 1, 1), ny, 8, 128), F32),
+            vmem((nz, max(ny - 1, 1), nx, 8, 128), F32),
+            vmem((nz, ny, 8, 128), F32),
+            vmem((nz, nx, 8, 128), F32),
+            vmem((nz, max(ny - 1, 1), 8, 128), F32),
+            vmem((nz, max(nx - 1, 1), 8, 128), F32),
             vmem((nz, 2, 8, 128), F32),
-            vmem((nz - 1, 2, 8, 128), F32),
+            vmem((nz, 2, 8, 128), F32),
             vmem((2, 16, 128), F32),
             vmem((2, 16, 128), F32),
             vmem((ny * nx, 16, 128), F32),
@@ -344,7 +376,9 @@
             pltpu.SemaphoreType.DMA((2, CHUNKS)),
         ]
         most = max(nx, ny) - 1
-        for shape in ((groups, 2), (groups, 2, most), (groups, 2, most), (nz,), (nx * ny + nz,)):
+        units = len(UNITS[nz])
+        for shape in ((len(BATCHES[nz]), 2), (2, 2), (units, 2, most), (units, 2, most), (nz,),
+                      (nx * ny + nz,)):
             scratch += [pltpu.SemaphoreType.DMA(shape)] * 2
         whole = pl.BlockSpec(memory_space=pltpu.VMEM)
         summed, factors = pl.pallas_call(

time: 32.4 us -> 31.1 us (0.960)
  Pallas kernels: 31.6 us -> 30.4 us
    pallas_call x1, Pallas kernels: 30.7 us -> 29.5 us  [step(): pl.pallas_call(functools.partial(kernel, sizes, schedule), out_shape=(jax...]
where the time goes in v2:
time: 31.1 us; the launch traced here: 31 us
  Pallas kernels  30.4 us (98%)
  between operations  0.64 us (2%)
    pallas_call x1, Pallas kernels, step(): pl.pallas_call(functools.partial(kernel, sizes, schedule), out_shape=(jax...  29.5 us
    pallas_call x1, Pallas kernels, step(): pl.pallas_call(finish_kernel, out_shape=(jax.ShapeDtypeStruct((32, PROBES...  0.9 us

profile of v2, /device:TPU:1, one launch (start us, length us, event | category | flops | bytes accessed | tf_op | source)
XLA Modules:
  0.0 31.0 jit_solution(8577754307772900963)
XLA Ops:
  0.6 29.5 %range_finder.1 = (f32[16,128]{1,0:T(8,128)S(1)}, f32[64,128]{1,0:T(8,128)S(1)}) custom-call(bf16[512,8192]{1,0:T(8,128)(2,1)} %g_hbm.1, bf16[64,8192]{1,0:T(8,128)(2,1)} %bitcast.1), custom_call_target="tpu_custom_call" | custom-call | tf_op jit(solution)/shard_map/range_finder/pallas_call | solution.py:384
  30.1 0.9 %finish.1 = (f32[32,64]{1,0:T(8,128)}, f32[64,64]{1,0:T(8,128)}) custom-call(f32[16,128]{1,0:T(8,128)S(1)} %get-tuple-element.4.sum_ref, f32[64,128]{1,0:T(8,128)S(1)} %get-tuple-element.5.work_ref), custom_call_target="tpu_custom_call" | custom-call | tf_op jit(solution)/shard_map/finish/pallas_call | solution.py:398

commit v3 on v2

--- a/solution.py
+++ b/solution.py
@@ -74,7 +74,7 @@
         )
 
 
-def kernel(sizes, schedule, g_hbm, p_hbm, sum_ref, work_ref, g_buf, p_buf, split, ya, yb, ca, cb,
+def kernel(sizes, schedule, g_hbm, p_hbm, sum_ref, work_ref, g_buf, p_buf, sketch_ref, split, ya, yb, ca, cb,
            za, zb, ra1, rb1, sa1, sb1, ra2, rb2, total2, rz, gram_own, gram_c, gram_xy, gram_z, gram_all, work,
            load_sem, core_send, core_recv, along_send, along_recv, one_send, one_recv, two_send, two_recv,
            z_send, z_recv, gram_send, gram_recv):
@@ -117,15 +117,15 @@
     for peer in peers:
         pl.semaphore_signal(barrier, inc=1, device_id=peer, device_id_type=MESH)
 
-    sketch = jnp.zeros((PROBES, g_hbm.shape[0]), F32)
     for j in range(CHUNKS):
         for load in loads[j]:
             load.wait()
         if j + DEPTH < CHUNKS:
             for load in loads[j + DEPTH]:
                 load.start()
-        sketch += lax.dot_general(p_buf[part(j)], g_buf[part(j)], NT, preferred_element_type=F32)
-    pieces = split3(sketch)
+        term = lax.dot_general(p_buf[part(j)], g_buf[part(j)], NT, preferred_element_type=F32)
+        sketch_ref[...] = sketch_ref[...] + term if j else term
+    pieces = split3(sketch_ref[...])
     for i, piece in enumerate(pieces):
         split[pl.ds(i * PROBES, PROBES)] = piece
 
@@ -352,6 +352,7 @@
         scratch = [
             vmem((samples, markers), BF16),
             vmem((PROBES, markers), BF16),
+            vmem((PROBES, samples), F32),
             vmem((3 * PROBES, samples), BF16),
             vmem((2, nz, nx, ny, 8, 128), F32),
             vmem((2, nz, ny, nx, 8, 128), F32),

time: 31.1 us -> 31.1 us (level)
  no operation moved by 1% of the time
where the time goes in v3:
time: 31.1 us; the launch traced here: 31 us
  Pallas kernels  30.3 us (97%)
  between operations  0.64 us (2%)
    pallas_call x1, Pallas kernels, step(): pl.pallas_call(functools.partial(kernel, sizes, schedule), out_shape=(jax...  29.4 us
    pallas_call x1, Pallas kernels, step(): pl.pallas_call(finish_kernel, out_shape=(jax.ShapeDtypeStruct((32, PROBES...  0.9 us

profile of v3, /device:TPU:1, one launch (start us, length us, event | category | flops | bytes accessed | tf_op | source)
XLA Modules:
  0.0 31.0 jit_solution(15924847831228544951)
XLA Ops:
  0.6 29.4 %range_finder.1 = (f32[16,128]{1,0:T(8,128)S(1)}, f32[64,128]{1,0:T(8,128)S(1)}) custom-call(bf16[512,8192]{1,0:T(8,128)(2,1)} %g_hbm.1, bf16[64,8192]{1,0:T(8,128)(2,1)} %bitcast.1), custom_call_target="tpu_custom_call" | custom-call | tf_op jit(solution)/shard_map/range_finder/pallas_call | solution.py:385
  30.1 0.9 %finish.1 = (f32[32,64]{1,0:T(8,128)}, f32[64,64]{1,0:T(8,128)}) custom-call(f32[16,128]{1,0:T(8,128)S(1)} %get-tuple-element.4.sum_ref, f32[64,128]{1,0:T(8,128)S(1)} %get-tuple-element.5.work_ref), custom_call_target="tpu_custom_call" | custom-call | tf_op jit(solution)/shard_map/finish/pallas_call | solution.py:399
